TPU v7x, 32 devices: a whole 2x2x4 slice. The times are simulated.
32 devices in a mesh: hi: 4 (over y, core), lo: 8 (over z, x).
Axes of the slice: x: 2, y: 2, z: 4, core: 2. Of those that a mesh axis runs over, the one named last changes fastest.
Arguments:
- vectors: bfloat16 [128, 65536], P(None, ('hi', 'lo')), may hold values from -6 to 6
- leaves: bfloat16 [65536, 512], P(('hi', 'lo')), may hold values from -0.25 to 0.25
- u_local: bfloat16 [2, 65536, 128], P(None, ('hi', 'lo')), may hold values from -0.5 to 0.5
- v_local: bfloat16 [2, 65536, 128], P(None, ('hi', 'lo')), may hold values from -6 to 6
- u_upper: bfloat16 [5, 65536, 128], P(None, ('hi', 'lo')), may hold values from -0.5 to 0.5
- v_upper: bfloat16 [5, 65536, 128], P(None, ('hi', 'lo')), may hold values from -6 to 6
Outputs:
- krylov_last: bfloat16 [128, 65536], P(None, ('hi', 'lo'))
All inputs are finite; a program needn't handle non-finite values.
Results may differ from a plain program's by a relative error of at most 0.018.
Values sent between devices are 32-bit elements; how exact they have to be, the bound alone decides.
A program may use at most 64 MiB of HBM per device.

v0:
```python
import math

import jax
import jax.numpy as jnp
from jax import lax
from jax.sharding import PartitionSpec as P

ITERS = 4


def from_partner(value, axis, distance):
    mask = 2**distance
    pairs = [(source, source ^ mask) for source in range(lax.axis_size(axis))]
    return lax.ppermute(value, axis, pairs)


def lower_steps(stack, lo_bits):
    found = []
    carried = stack
    for level_bit in range(lo_bits):
        arrived = from_partner(carried, "lo", level_bit)
        found.append(arrived[0])
        carried = carried[1:] + arrived[1:]
    return (found, carried)


def upper_sums(hi_parts, hi_bits):
    found = []
    carried = hi_parts
    for level_bit in range(hi_bits):
        arrived = from_partner(carried, "hi", level_bit)
        found.append(arrived[0])
        carried = carried[1:] + arrived[1:]
    return found


def apply_operator(state, leaves, u_local, v_local, u_upper, v_upper):
    wide, dev_rows = state.shape
    leaf_rows = leaves.shape[1]
    local_count = u_local.shape[0]
    upper_count = u_upper.shape[0]
    level_count = local_count + upper_count
    lo_bits = lax.axis_size("lo").bit_length() - 1
    hi_bits = lax.axis_size("hi").bit_length() - 1
    rank_cols = u_local.shape[2]
    parts = jnp.einsum("bsr,cs->bcr", v_upper, state, preferred_element_type=jnp.float32)
    lower_found, hi_parts = lower_steps(parts, lo_bits)
    blocks = leaves.reshape(dev_rows // leaf_rows, leaf_rows, leaf_rows)
    result = jnp.einsum(
        "gij,cgj->cgi",
        blocks,
        state.reshape(wide, dev_rows // leaf_rows, leaf_rows),
        preferred_element_type=jnp.float32,
    ).reshape(wide, dev_rows)
    for level in range(local_count):
        node_rows = leaf_rows * 2**level
        groups = dev_rows // node_rows
        coef = jnp.einsum(
            "gsr,cgs->gcr",
            v_local[level].reshape(groups, node_rows, rank_cols),
            state.reshape(wide, groups, node_rows),
            preferred_element_type=jnp.float32,
        )
        coef = coef.reshape(groups // 2, 2, wide, rank_cols)[:, ::-1].reshape(
            groups, wide, rank_cols
        )
        coef = (coef * (1.0 / math.sqrt(node_rows * level_count))).astype(jnp.bfloat16)
        added = jnp.einsum(
            "gsr,gcr->cgs",
            u_local[level].reshape(groups, node_rows, rank_cols),
            coef,
            preferred_element_type=jnp.float32,
        )
        result = result + added.reshape(wide, dev_rows)
    upper_found = upper_sums(hi_parts, hi_bits)
    coefs = jnp.stack(lower_found + upper_found)
    factors = jnp.array(
        [
            1.0 / math.sqrt(dev_rows * 2**level_bit * level_count)
            for level_bit in range(upper_count)
        ],
        dtype=jnp.float32,
    )
    coefs = (coefs * factors[:, None, None]).astype(jnp.bfloat16)
    result = result + jnp.einsum("bsr,bcr->cs", u_upper, coefs, preferred_element_type=jnp.float32)
    return result.astype(jnp.bfloat16)


def local(vectors, leaves, u_local, v_local, u_upper, v_upper):
    state = vectors
    for step in range(ITERS):
        state = apply_operator(state, leaves, u_local, v_local, u_upper, v_upper)
    return state


def solution(mesh):
    return jax.shard_map(
        local,
        mesh=mesh,
        in_specs=(
            P(None, ("hi", "lo")),
            P(("hi", "lo"), None),
            P(None, ("hi", "lo"), None),
            P(None, ("hi", "lo"), None),
            P(None, ("hi", "lo"), None),
            P(None, ("hi", "lo"), None),
        ),
        out_specs=P(None, ("hi", "lo")),
        check_vma=False,
    )
```

profile of v0, /device:TPU:0, one launch (start us, length us, event | category | flops | bytes accessed | tf_op | source)
XLA Modules:
  0.0 191.8 jit_solution(12566042129857140843)
XLA Ops:
  0.0 2.6 %convolution_bitcast_fusion.11 = f32[5,128,128]{2,1,0:T(8,128)S(1)} fusion(bf16[5,2048,128]{2,1,0:T(8,128)(2,1)} %param.15, bf16[128,2048]{1,0:T(8,128)(2,1)} %param.10), kind=kOutput, calls=%fused_computation.27 | convolution fusion | flops 335544320 | bytes 3473408 | tf_op jit(solution)/shard_map/bsr,cs->bcr/dot_general | solution.py:46
  2.7 3.0 %collective-permute-start = (f32[5,128,128]{2,1,0:T(8,128)S(1)}, f32[5,128,128]{2,1,0:T(8,128)S(1)}, u32[]{:S(2)}, u32[]{:S(2)}) collective-permute-start(f32[5,128,128]{2,1,0:T(8,128)S(1)} %convolution_bitcast_fusion.11), channel_id=1, source_target_pairs={{0,1},{1,0},{2,3},{3,2},{4,5},{5,4},{6,7},{7,6},{8,9},{9,8},{10,11... | collective-permute-start | bytes 983048 | tf_op jit(solution)/shard_map/ppermute | solution.py:14
  8.7 4.7 %collective-permute-done = f32[5,128,128]{2,1,0:T(8,128)S(1)} collective-permute-done((f32[5,128,128]{2,1,0:T(8,128)S(1)}, f32[5,128,128]{2,1,0:T(8,128)S(1)}, u32[]{:S(2)}, u32[]{:S(2)}) %collective-permute-start) | collective-permute-done | bytes 327712 | tf_op jit(solution)/shard_map/ppermute | solution.py:14
  15.3 5.6 %collective-permute-done.1 = f32[4,128,128]{2,1,0:T(8,128)S(1)} collective-permute-done((f32[4,128,128]{2,1,0:T(8,128)S(1)}, f32[4,128,128]{2,1,0:T(8,128)S(1)}, u32[]{:S(2)}, u32[]{:S(2)}) %collective-permute-start.1) | collective-permute-done | bytes 262176 | tf_op jit(solution)/shard_map/ppermute | solution.py:14
  21.0 2.6 %collective-permute-start.2 = (f32[3,128,128]{2,1,0:T(8,128)S(1)}, f32[3,128,128]{2,1,0:T(8,128)S(1)}, u32[]{:S(2)}, u32[]{:S(2)}) collective-permute-start(f32[3,128,128]{2,1,0:T(8,128)S(1)} %slice_add_fusion.7), channel_id=1, source_target_pairs={{0,4},{1,5},{2,6},{3,7},{4,0},{5,1},{6,2},{7,3},{8,12},{9,13},{10,... | collective-permute-start | bytes 589832 | tf_op jit(solution)/shard_map/ppermute | solution.py:14
  23.6 7.7 %collective-permute-done.2 = f32[3,128,128]{2,1,0:T(8,128)S(1)} collective-permute-done((f32[3,128,128]{2,1,0:T(8,128)S(1)}, f32[3,128,128]{2,1,0:T(8,128)S(1)}, u32[]{:S(2)}, u32[]{:S(2)}) %collective-permute-start.2) | collective-permute-done | bytes 196640 | tf_op jit(solution)/shard_map/ppermute | solution.py:14
  37.8 2.6 %copy.23 = f32[128,2048]{1,0:T(8,128)} copy(f32[128,2048]{0,1:T(8,128)} %bitcast.185) | data formatting | bytes 2097152 | tf_op jit(solution)/shard_map/add | solution.py:74
  40.4 2.5 %copy.22 = f32[128,2,1024]{0,2,1:T(8,128)} copy(f32[128,2,1024]{2,0,1:T(8,128)} %convolution_bitcast_fusion.7) | data formatting | bytes 2097152 | tf_op jit(solution)/shard_map/gsr,gcr->cgs/transpose | solution.py:68
  42.9 2.6 %copy.24 = f32[128,2048]{1,0:T(8,128)} copy(f32[128,2048]{0,1:T(8,128)} %bitcast.186) | data formatting | bytes 2097152 | tf_op jit(solution)/shard_map/reshape | solution.py:74
  46.3 2.6 %fusion.7 = bf16[128,2048]{1,0:T(8,128)(2,1)S(1)} fusion(bf16[5,2048,128]{2,1,0:T(8,128)(2,1)S(1)} %copy-done, f32[128,2048]{1,0:T(8,128)} %copy.23, f32[128,2048]{1,0:T(8,128)} %copy.24, f32[5,128,128]{2,1,0:T(8,128)S(1)} %constant_dynamic-update-slice_fusion, f32[5]{0:T(128)S(1)} %copy-done.23), kind=kOutput, calls=%fused_computation.11 | convolution fusion | flops 336494592 | bytes 5570580 | tf_op jit(solution)/shard_map/bsr,bcr->cs/dot_general | solution.py:85
  54.8 6.7 %collective-permute-done.5 = f32[5,128,128]{2,1,0:T(8,128)S(1)} collective-permute-done((f32[5,128,128]{2,1,0:T(8,128)S(1)}, f32[5,128,128]{2,1,0:T(8,128)S(1)}, u32[]{:S(2)}, u32[]{:S(2)}) %collective-permute-start.5) | collective-permute-done | bytes 327712 | tf_op jit(solution)/shard_map/ppermute | solution.py:14
  62.3 6.5 %collective-permute-done.6 = f32[4,128,128]{2,1,0:T(8,128)S(1)} collective-permute-done((f32[4,128,128]{2,1,0:T(8,128)S(1)}, f32[4,128,128]{2,1,0:T(8,128)S(1)}, u32[]{:S(2)}, u32[]{:S(2)}) %collective-permute-start.6) | collective-permute-done | bytes 262176 | tf_op jit(solution)/shard_map/ppermute | solution.py:14
  71.2 7.7 %collective-permute-done.7 = f32[3,128,128]{2,1,0:T(8,128)S(1)} collective-permute-done((f32[3,128,128]{2,1,0:T(8,128)S(1)}, f32[3,128,128]{2,1,0:T(8,128)S(1)}, u32[]{:S(2)}, u32[]{:S(2)}) %collective-permute-start.7) | collective-permute-done | bytes 196640 | tf_op jit(solution)/shard_map/ppermute | solution.py:14
  82.6 2.5 %copy.28 = f32[128,2,1024]{0,2,1:T(8,128)} copy(f32[128,2,1024]{2,0,1:T(8,128)} %convolution_bitcast_fusion.6) | data formatting | bytes 2097152 | tf_op jit(solution)/shard_map/gsr,gcr->cgs/transpose | solution.py:68
  85.1 2.6 %copy.30 = f32[128,2048]{1,0:T(8,128)} copy(f32[128,2048]{0,1:T(8,128)} %bitcast.187) | data formatting | bytes 2097152 | tf_op jit(solution)/shard_map/reshape | solution.py:74
  87.7 2.5 %copy.27 = f32[128,4,512]{0,2,1:T(8,128)} copy(f32[128,4,512]{2,0,1:T(8,128)} %fusion.10) | data formatting | bytes 2097152 | tf_op jit(solution)/shard_map/add | solution.py:74
  90.2 2.6 %copy.29 = f32[128,2048]{1,0:T(8,128)} copy(f32[128,2048]{0,1:T(8,128)} %bitcast.188) | data formatting | bytes 2097152 | tf_op jit(solution)/shard_map/add | solution.py:74
  93.6 2.6 %fusion.6 = bf16[128,2048]{1,0:T(8,128)(2,1)S(1)} fusion(bf16[5,2048,128]{2,1,0:T(8,128)(2,1)S(1)} %copy-done, f32[128,2048]{1,0:T(8,128)} %copy.29, f32[128,2048]{1,0:T(8,128)} %copy.30, f32[5,128,128]{2,1,0:T(8,128)S(1)} %constant_dynamic-update-slice_fusion.1, f32[5]{0:T(128)S(1)} %copy-done.23), kind=kOutput, calls=%fused_computation.10 | convolution fusion | flops 336494592 | bytes 5570580 | tf_op jit(solution)/shard_map/bsr,bcr->cs/dot_general | solution.py:85
  101.7 7.0 %collective-permute-done.10 = f32[5,128,128]{2,1,0:T(8,128)S(1)} collective-permute-done((f32[5,128,128]{2,1,0:T(8,128)S(1)}, f32[5,128,128]{2,1,0:T(8,128)S(1)}, u32[]{:S(2)}, u32[]{:S(2)}) %collective-permute-start.10) | collective-permute-done | bytes 327712 | tf_op jit(solution)/shard_map/ppermute | solution.py:14
  109.1 6.9 %collective-permute-done.11 = f32[4,128,128]{2,1,0:T(8,128)S(1)} collective-permute-done((f32[4,128,128]{2,1,0:T(8,128)S(1)}, f32[4,128,128]{2,1,0:T(8,128)S(1)}, u32[]{:S(2)}, u32[]{:S(2)}) %collective-permute-start.11) | collective-permute-done | bytes 262176 | tf_op jit(solution)/shard_map/ppermute | solution.py:14
  118.1 8.1 %collective-permute-done.12 = f32[3,128,128]{2,1,0:T(8,128)S(1)} collective-permute-done((f32[3,128,128]{2,1,0:T(8,128)S(1)}, f32[3,128,128]{2,1,0:T(8,128)S(1)}, u32[]{:S(2)}, u32[]{:S(2)}) %collective-permute-start.12) | collective-permute-done | bytes 196640 | tf_op jit(solution)/shard_map/ppermute | solution.py:14
  130.1 2.5 %copy.34 = f32[128,2,1024]{0,2,1:T(8,128)} copy(f32[128,2,1024]{2,0,1:T(8,128)} %convolution_bitcast_fusion.5) | data formatting | bytes 2097152 | tf_op jit(solution)/shard_map/gsr,gcr->cgs/transpose | solution.py:68
  132.6 2.6 %copy.36 = f32[128,2048]{1,0:T(8,128)} copy(f32[128,2048]{0,1:T(8,128)} %bitcast.189) | data formatting | bytes 2097152 | tf_op jit(solution)/shard_map/reshape | solution.py:74
  135.2 2.5 %copy.33 = f32[128,4,512]{0,2,1:T(8,128)} copy(f32[128,4,512]{2,0,1:T(8,128)} %fusion.9) | data formatting | bytes 2097152 | tf_op jit(solution)/shard_map/add | solution.py:74
  137.7 2.6 %copy.35 = f32[128,2048]{1,0:T(8,128)} copy(f32[128,2048]{0,1:T(8,128)} %bitcast.190) | data formatting | bytes 2097152 | tf_op jit(solution)/shard_map/add | solution.py:74
  141.1 2.8 %fusion.5 = bf16[128,2048]{1,0:T(8,128)(2,1)S(1)} fusion(bf16[5,2048,128]{2,1,0:T(8,128)(2,1)S(1)} %copy-done, f32[128,2048]{1,0:T(8,128)} %copy.35, f32[128,2048]{1,0:T(8,128)} %copy.36, f32[5,128,128]{2,1,0:T(8,128)S(1)} %constant_dynamic-update-slice_fusion.2, f32[5]{0:T(128)S(1)} %copy-done.23), kind=kOutput, calls=%fused_computation.9 | convolution fusion | flops 336494592 | bytes 5570580 | tf_op jit(solution)/shard_map/bsr,bcr->cs/dot_general | solution.py:85
  149.7 6.7 %collective-permute-done.15 = f32[5,128,128]{2,1,0:T(8,128)S(1)} collective-permute-done((f32[5,128,128]{2,1,0:T(8,128)S(1)}, f32[5,128,128]{2,1,0:T(8,128)S(1)}, u32[]{:S(2)}, u32[]{:S(2)}) %collective-permute-start.15) | collective-permute-done | bytes 327712 | tf_op jit(solution)/shard_map/ppermute | solution.py:14
  157.2 6.5 %collective-permute-done.16 = f32[4,128,128]{2,1,0:T(8,128)S(1)} collective-permute-done((f32[4,128,128]{2,1,0:T(8,128)S(1)}, f32[4,128,128]{2,1,0:T(8,128)S(1)}, u32[]{:S(2)}, u32[]{:S(2)}) %collective-permute-start.16) | collective-permute-done | bytes 262176 | tf_op jit(solution)/shard_map/ppermute | solution.py:14
  166.1 7.7 %collective-permute-done.17 = f32[3,128,128]{2,1,0:T(8,128)S(1)} collective-permute-done((f32[3,128,128]{2,1,0:T(8,128)S(1)}, f32[3,128,128]{2,1,0:T(8,128)S(1)}, u32[]{:S(2)}, u32[]{:S(2)}) %collective-permute-start.17) | collective-permute-done | bytes 196640 | tf_op jit(solution)/shard_map/ppermute | solution.py:14
  180.0 2.6 %copy.42 = f32[128,2048]{1,0:T(8,128)} copy(f32[128,2048]{0,1:T(8,128)} %bitcast.191) | data formatting | bytes 2097152 | tf_op jit(solution)/shard_map/reshape | solution.py:74
  185.1 2.6 %copy.41 = f32[128,2048]{1,0:T(8,128)} copy(f32[128,2048]{0,1:T(8,128)} %bitcast.192) | data formatting | bytes 2097152 | tf_op jit(solution)/shard_map/add | solution.py:74
  188.5 3.3 %fusion.4 = bf16[128,2048]{1,0:T(8,128)(2,1)} fusion(bf16[5,2048,128]{2,1,0:T(8,128)(2,1)S(1)} %copy-done, f32[128,2048]{1,0:T(8,128)} %copy.41, f32[128,2048]{1,0:T(8,128)} %copy.42, f32[5,128,128]{2,1,0:T(8,128)S(1)} %constant_dynamic-update-slice_fusion.3, f32[5]{0:T(128)S(1)} %copy-done.23), kind=kOutput, calls=%fused_computation.8 | convolution fusion | flops 336494592 | bytes 5570580 | tf_op jit(solution)/shard_map/bsr,bcr->cs/dot_general | solution.py:85
  (142 shorter events, 56.6 us)
Async XLA Ops:
  0.0 46.3 %copy-start = (bf16[5,2048,128]{2,1,0:T(8,128)(2,1)S(1)}, bf16[5,2048,128]{2,1,0:T(8,128)(2,1)}, u32[]{:S(2)}) copy-start(bf16[5,2048,128]{2,1,0:T(8,128)(2,1)} %param.14) | copy-start | bytes 7864324
  0.0 5.7 %copy-start.17 = (bf16[2,2048,128]{2,1,0:T(8,128)(2,1)S(1)}, bf16[2,2048,128]{2,1,0:T(8,128)(2,1)}, u32[]{:S(2)}) copy-start(bf16[2,2048,128]{2,1,0:T(8,128)(2,1)} %param.12) | copy-start | bytes 3145732
  0.0 5.7 %copy-start.18 = (bf16[2,2048,128]{2,1,0:T(8,128)(2,1)S(1)}, bf16[2,2048,128]{2,1,0:T(8,128)(2,1)}, u32[]{:S(2)}) copy-start(bf16[2,2048,128]{2,1,0:T(8,128)(2,1)} %param.13) | copy-start | bytes 3145732
  2.6 3.2 %copy-start.4 = (bf16[2048,512]{1,0:T(8,128)(2,1)S(1)}, bf16[2048,512]{1,0:T(8,128)(2,1)}, u32[]{:S(2)}) copy-start(bf16[2048,512]{1,0:T(8,128)(2,1)} %param.11) | copy-start | bytes 6291460
  2.7 3.2 %copy-start.16 = (bf16[128,2048]{1,0:T(8,128)(2,1)S(1)}, bf16[128,2048]{1,0:T(8,128)(2,1)}, u32[]{:S(2)}) copy-start(bf16[128,2048]{1,0:T(8,128)(2,1)} %param.10) | copy-start | bytes 1572868
  2.7 10.7 %collective-permute-start = (f32[5,128,128]{2,1,0:T(8,128)S(1)}, f32[5,128,128]{2,1,0:T(8,128)S(1)}, u32[]{:S(2)}, u32[]{:S(2)}) collective-permute-start(f32[5,128,128]{2,1,0:T(8,128)S(1)} %convolution_bitcast_fusion.11), channel_id=1, source_target_pairs={{0,1},{1,0},{2,3},{3,2},{4,5},{5,4},{6,7},{7,6},{8,9},{9,8},{10,11... | collective-permute-start | bytes 983048 | tf_op jit(solution)/shard_map/ppermute | solution.py:14
  13.4 7.6 %collective-permute-start.1 = (f32[4,128,128]{2,1,0:T(8,128)S(1)}, f32[4,128,128]{2,1,0:T(8,128)S(1)}, u32[]{:S(2)}, u32[]{:S(2)}) collective-permute-start(f32[4,128,128]{2,1,0:T(8,128)S(1)} %slice_add_fusion.3), channel_id=1, source_target_pairs={{0,2},{1,3},{2,0},{3,1},{4,6},{5,7},{6,4},{7,5},{8,10},{9,11},{10,... | collective-permute-start | bytes 786440 | tf_op jit(solution)/shard_map/ppermute | solution.py:14
  21.0 10.3 %collective-permute-start.2 = (f32[3,128,128]{2,1,0:T(8,128)S(1)}, f32[3,128,128]{2,1,0:T(8,128)S(1)}, u32[]{:S(2)}, u32[]{:S(2)}) collective-permute-start(f32[3,128,128]{2,1,0:T(8,128)S(1)} %slice_add_fusion.7), channel_id=1, source_target_pairs={{0,4},{1,5},{2,6},{3,7},{4,0},{5,1},{6,2},{7,3},{8,12},{9,13},{10,... | collective-permute-start | bytes 589832 | tf_op jit(solution)/shard_map/ppermute | solution.py:14
  31.4 1.4 collective-permute-start.3
  32.8 12.7 %collective-permute-start.4 = (f32[1,128,128]{2,1,0:T(8,128)S(1)}, f32[1,128,128]{2,1,0:T(8,128)}, u32[]{:S(2)}, u32[]{:S(2)}) collective-permute-start(f32[1,128,128]{2,1,0:T(8,128)S(1)} %get-tuple-element.15), channel_id=1, source_target_pairs={{0,16},{8,24},{16,0},{24,8},{1,17},{9,25},{17,1},{25,9},{2,18},{10... | collective-permute-start | bytes 196616 | tf_op jit(solution)/shard_map/ppermute | solution.py:14
  40.4 6.0 %copy-start.23 = (f32[5]{0:T(128)S(1)}, f32[5]{0:T(128)}, u32[]{:S(2)}) copy-start(f32[5]{0:T(128)} %constant.6.clone) | copy-start | bytes 64
  46.3 2.7 %copy-start.1 = (bf16[5,2048,128]{2,1,0:T(8,128)(2,1)S(1)}, bf16[5,2048,128]{2,1,0:T(8,128)(2,1)}, u32[]{:S(2)}) copy-start(bf16[5,2048,128]{2,1,0:T(8,128)(2,1)} %param.15) | copy-start | bytes 7864324
  50.8 2.7 %copy-start.13 = (bf16[1,2048,128]{2,1,0:T(8,128)(2,1)S(1)}, bf16[1,2048,128]{2,1,0:T(8,128)(2,1)}, u32[]{:S(2)}) copy-start(bf16[1,2048,128]{2,1,0:T(8,128)(2,1)} %copy-done.12) | copy-start | bytes 1572868
  51.9 9.6 %collective-permute-start.5 = (f32[5,128,128]{2,1,0:T(8,128)S(1)}, f32[5,128,128]{2,1,0:T(8,128)S(1)}, u32[]{:S(2)}, u32[]{:S(2)}) collective-permute-start(f32[5,128,128]{2,1,0:T(8,128)S(1)} %convolution_bitcast_fusion.10), channel_id=1, source_target_pairs={{0,1},{1,0},{2,3},{3,2},{4,5},{5,4},{6,7},{7,6},{8,9},{9,8},{10,11... | collective-permute-start | bytes 983048 | tf_op jit(solution)/shard_map/ppermute | solution.py:14
  61.5 7.3 %collective-permute-start.6 = (f32[4,128,128]{2,1,0:T(8,128)S(1)}, f32[4,128,128]{2,1,0:T(8,128)S(1)}, u32[]{:S(2)}, u32[]{:S(2)}) collective-permute-start(f32[4,128,128]{2,1,0:T(8,128)S(1)} %slice_add_fusion.2), channel_id=1, source_target_pairs={{0,2},{1,3},{2,0},{3,1},{4,6},{5,7},{6,4},{7,5},{8,10},{9,11},{10,... | collective-permute-start | bytes 786440 | tf_op jit(solution)/shard_map/ppermute | solution.py:14
  68.8 10.1 %collective-permute-start.7 = (f32[3,128,128]{2,1,0:T(8,128)S(1)}, f32[3,128,128]{2,1,0:T(8,128)S(1)}, u32[]{:S(2)}, u32[]{:S(2)}) collective-permute-start(f32[3,128,128]{2,1,0:T(8,128)S(1)} %slice_add_fusion.6), channel_id=1, source_target_pairs={{0,4},{1,5},{2,6},{3,7},{4,0},{5,1},{6,2},{7,3},{8,12},{9,13},{10,... | collective-permute-start | bytes 589832 | tf_op jit(solution)/shard_map/ppermute | solution.py:14
  78.9 1.4 collective-permute-start.8
  80.3 12.4 %collective-permute-start.9 = (f32[1,128,128]{2,1,0:T(8,128)S(1)}, f32[1,128,128]{2,1,0:T(8,128)}, u32[]{:S(2)}, u32[]{:S(2)}) collective-permute-start(f32[1,128,128]{2,1,0:T(8,128)S(1)} %get-tuple-element.13), channel_id=1, source_target_pairs={{0,16},{8,24},{16,0},{24,8},{1,17},{9,25},{17,1},{25,9},{2,18},{10... | collective-permute-start | bytes 196616 | tf_op jit(solution)/shard_map/ppermute | solution.py:14
  93.6 2.7 %copy-start.2 = (bf16[5,2048,128]{2,1,0:T(8,128)(2,1)S(1)}, bf16[5,2048,128]{2,1,0:T(8,128)(2,1)}, u32[]{:S(2)}) copy-start(bf16[5,2048,128]{2,1,0:T(8,128)(2,1)} %param.15) | copy-start | bytes 7864324
  98.0 2.3 %copy-start.14 = (bf16[1,2048,128]{2,1,0:T(8,128)(2,1)S(1)}, bf16[1,2048,128]{2,1,0:T(8,128)(2,1)}, u32[]{:S(2)}) copy-start(bf16[1,2048,128]{2,1,0:T(8,128)(2,1)} %copy-done.12) | copy-start | bytes 1572868
  99.2 9.6 %collective-permute-start.10 = (f32[5,128,128]{2,1,0:T(8,128)S(1)}, f32[5,128,128]{2,1,0:T(8,128)S(1)}, u32[]{:S(2)}, u32[]{:S(2)}) collective-permute-start(f32[5,128,128]{2,1,0:T(8,128)S(1)} %convolution_bitcast_fusion.9), channel_id=1, source_target_pairs={{0,1},{1,0},{2,3},{3,2},{4,5},{5,4},{6,7},{7,6},{8,9},{9,8},{10,11... | collective-permute-start | bytes 983048 | tf_op jit(solution)/shard_map/ppermute | solution.py:14
  108.8 7.3 %collective-permute-start.11 = (f32[4,128,128]{2,1,0:T(8,128)S(1)}, f32[4,128,128]{2,1,0:T(8,128)S(1)}, u32[]{:S(2)}, u32[]{:S(2)}) collective-permute-start(f32[4,128,128]{2,1,0:T(8,128)S(1)} %slice_add_fusion.1), channel_id=1, source_target_pairs={{0,2},{1,3},{2,0},{3,1},{4,6},{5,7},{6,4},{7,5},{8,10},{9,11},{10,... | collective-permute-start | bytes 786440 | tf_op jit(solution)/shard_map/ppermute | solution.py:14
  116.1 10.1 %collective-permute-start.12 = (f32[3,128,128]{2,1,0:T(8,128)S(1)}, f32[3,128,128]{2,1,0:T(8,128)S(1)}, u32[]{:S(2)}, u32[]{:S(2)}) collective-permute-start(f32[3,128,128]{2,1,0:T(8,128)S(1)} %slice_add_fusion.5), channel_id=1, source_target_pairs={{0,4},{1,5},{2,6},{3,7},{4,0},{5,1},{6,2},{7,3},{8,12},{9,13},{10,... | collective-permute-start | bytes 589832 | tf_op jit(solution)/shard_map/ppermute | solution.py:14
  126.1 1.4 collective-permute-start.13
  127.6 12.7 %collective-permute-start.14 = (f32[1,128,128]{2,1,0:T(8,128)S(1)}, f32[1,128,128]{2,1,0:T(8,128)}, u32[]{:S(2)}, u32[]{:S(2)}) collective-permute-start(f32[1,128,128]{2,1,0:T(8,128)S(1)} %get-tuple-element.11), channel_id=1, source_target_pairs={{0,16},{8,24},{16,0},{24,8},{1,17},{9,25},{17,1},{25,9},{2,18},{10... | collective-permute-start | bytes 196616 | tf_op jit(solution)/shard_map/ppermute | solution.py:14
  141.1 2.8 %copy-start.3 = (bf16[5,2048,128]{2,1,0:T(8,128)(2,1)S(1)}, bf16[5,2048,128]{2,1,0:T(8,128)(2,1)}, u32[]{:S(2)}) copy-start(bf16[5,2048,128]{2,1,0:T(8,128)(2,1)} %param.15) | copy-start | bytes 7864324
  145.7 2.7 %copy-start.15 = (bf16[1,2048,128]{2,1,0:T(8,128)(2,1)S(1)}, bf16[1,2048,128]{2,1,0:T(8,128)(2,1)}, u32[]{:S(2)}) copy-start(bf16[1,2048,128]{2,1,0:T(8,128)(2,1)} %copy-done.12) | copy-start | bytes 1572868
  146.8 9.6 %collective-permute-start.15 = (f32[5,128,128]{2,1,0:T(8,128)S(1)}, f32[5,128,128]{2,1,0:T(8,128)S(1)}, u32[]{:S(2)}, u32[]{:S(2)}) collective-permute-start(f32[5,128,128]{2,1,0:T(8,128)S(1)} %convolution_bitcast_fusion.8), channel_id=1, source_target_pairs={{0,1},{1,0},{2,3},{3,2},{4,5},{5,4},{6,7},{7,6},{8,9},{9,8},{10,11... | collective-permute-start | bytes 983048 | tf_op jit(solution)/shard_map/ppermute | solution.py:14
  156.4 7.3 %collective-permute-start.16 = (f32[4,128,128]{2,1,0:T(8,128)S(1)}, f32[4,128,128]{2,1,0:T(8,128)S(1)}, u32[]{:S(2)}, u32[]{:S(2)}) collective-permute-start(f32[4,128,128]{2,1,0:T(8,128)S(1)} %slice_add_fusion), channel_id=1, source_target_pairs={{0,2},{1,3},{2,0},{3,1},{4,6},{5,7},{6,4},{7,5},{8,10},{9,11},{10,... | collective-permute-start | bytes 786440 | tf_op jit(solution)/shard_map/ppermute | solution.py:14
  163.7 10.1 %collective-permute-start.17 = (f32[3,128,128]{2,1,0:T(8,128)S(1)}, f32[3,128,128]{2,1,0:T(8,128)S(1)}, u32[]{:S(2)}, u32[]{:S(2)}) collective-permute-start(f32[3,128,128]{2,1,0:T(8,128)S(1)} %slice_add_fusion.4), channel_id=1, source_target_pairs={{0,4},{1,5},{2,6},{3,7},{4,0},{5,1},{6,2},{7,3},{8,12},{9,13},{10,... | collective-permute-start | bytes 589832 | tf_op jit(solution)/shard_map/ppermute | solution.py:14
  173.8 1.4 collective-permute-start.18
  175.3 12.4 %collective-permute-start.19 = (f32[1,128,128]{2,1,0:T(8,128)S(1)}, f32[1,128,128]{2,1,0:T(8,128)}, u32[]{:S(2)}, u32[]{:S(2)}) collective-permute-start(f32[1,128,128]{2,1,0:T(8,128)S(1)} %get-tuple-element.9), channel_id=1, source_target_pairs={{0,16},{8,24},{16,0},{24,8},{1,17},{9,25},{17,1},{25,9},{2,18},{10... | collective-permute-start | bytes 196616 | tf_op jit(solution)/shard_map/ppermute | solution.py:14
  (12 other events, 18.8 us)
where the time goes:
time: 193 us; the launch traced here: 192 us
  waiting for transfers between devices  87.1 us (45%)
  local copies, waits for them, and re-layouts  47 us (24%)
  matrix products  31.7 us (16%)
  starting transfers between devices  24.9 us (13%)
    ppermute x20, waiting for transfers between devices, from_partner(): return lax.ppermute(value, axis, pairs)  87.1 us
    ppermute x20, starting transfers between devices, from_partner(): return lax.ppermute(value, axis, pairs)  24.9 us
    add x8, local copies, waits for them, and re-layouts, apply_operator(): result = result + added.reshape(wide, dev_rows)  20.3 us
    dot_general x4, matrix products, apply_operator(): jnp.einsum('bsr,bcr->cs', u_upper, coefs, preferred_element_type=jnp.floa...  11.4 us
    dot_general x8, matrix products, apply_operator(): jnp.einsum('gsr,gcr->cgs', u_local[level].reshape(groups, node_rows, rank...  10.4 us
    reshape x4, local copies, waits for them, and re-layouts, apply_operator(): result = result + added.reshape(wide, dev_rows)  10.2 us
    transpose x4, local copies, waits for them, and re-layouts, apply_operator(): jnp.einsum('gsr,gcr->cgs', u_local[level].reshape(groups, node_rows, rank...  10.1 us
    dot_general x4, matrix products, apply_operator(): jnp.einsum('bsr,cs->bcr', v_upper, state, preferred_element_type=jnp.floa...  4.38 us
  transfers between devices with their start and end apart: 20, of which 16 were waited for; matrix products, arithmetic and copies ran while one was open for 28% of the time, Pallas kernels for 0%

commit v1 on v0

v1 whole, which is shorter than its diff:
```python
import functools
import math

import jax
import jax.numpy as jnp
from jax import lax
from jax.experimental import pallas as pl
from jax.experimental.pallas import tpu as pltpu
from jax.sharding import PartitionSpec as P

ITERS = 4
GROUP_BITS = 3
CHUNKS = 1
MESH = pl.DeviceIdType.MESH
F32 = jnp.float32
BF16 = jnp.bfloat16


def flip(value, mask):
    bit = 0
    out = value
    while mask >> bit:
        if (mask >> bit) & 1:
            step = 2**bit
            out = out + step - 2 * step * lax.rem(lax.div(value, step), 2)
        bit += 1
    return out


class Plan:
    def __init__(self, levels, group_bits, wide):
        self.levels = levels
        self.k = min(group_bits, levels - 1)
        self.wide = wide
        k = self.k
        self.runs = [(b, 1, 2**b) for b in range(1, k)] + [(k, levels - k, 2**k)]
        self.first = [(r, m) for r, run in enumerate(self.runs) for m in range(1, run[2])]
        self.cross = [(b, m) for b in range(levels) for m in range(2 ** max(0, b - k))]
        self.slots2 = [(b, m) for b, m in self.cross if b > k]

    def rows(self, group):
        return self.wide // group

    def cross_mask(self, b, m):
        return (1 << b) ^ (m << self.k)

    def partners(self):
        masks = {m for _, m in self.first} | {self.cross_mask(b, m) for b, m in self.cross}
        return sorted(masks)


def nt(a, b):
    return lax.dot_general(a, b, (((1,), (1,)), ((), ())), preferred_element_type=F32)


def nn(a, b):
    return jnp.dot(a, b, preferred_element_type=F32)


def kernel(plan, lo_size, chunks, leaf_rows, *refs):
    hbm, o_ref = refs[:6], refs[6]
    leaves, u_loc, v_loc, u_up, v_up = refs[7:12]
    acc, parts, coef, recv2 = refs[12:16]
    recv1 = refs[16 : 16 + len(plan.runs)]
    load_sem, s1, r1, s2, r2, s3, r3 = refs[16 + len(plan.runs) :]
    levels, k = plan.levels, plan.k
    wide = plan.wide
    dev_rows = o_ref.shape[1]
    local_count = u_loc.shape[0]
    level_count = local_count + levels
    leaf_count = dev_rows // leaf_rows
    lo_bits = lo_size.bit_length() - 1

    dests = (o_ref, leaves, u_loc, v_loc, u_up, v_up)
    loads = [pltpu.make_async_copy(hbm[i], dests[i], load_sem.at[i]) for i in range(6)]
    for i in (0, 5, 1, 3, 2, 4):
        loads[i].start()

    hi = lax.axis_index("hi")
    lo = lax.axis_index("lo")
    me = hi * lo_size + lo

    def peer(mask):
        return (flip(hi, mask >> lo_bits), flip(lo, mask & (lo_size - 1)))

    barrier = pltpu.get_barrier_semaphore()
    masks = plan.partners()
    for mask in masks:
        pl.semaphore_signal(barrier, inc=1, device_id=peer(mask), device_id_type=MESH)
    loads[0].wait()
    loads[5].wait()
    pl.semaphore_wait(barrier, len(masks))

    def piece(group, mask):
        rows = plan.rows(group)
        index = flip(lax.rem(me, group), mask)
        return pl.ds(pl.multiple_of(index * rows, 8), rows)

    def copy1(slot, i):
        run, m = plan.first[i]
        b, count, group = plan.runs[run]
        return pltpu.make_async_remote_copy(
            src_ref=parts.at[slot, pl.ds(b, count), piece(group, m)],
            dst_ref=recv1[run].at[slot, m - 1],
            send_sem=s1.at[slot, i],
            recv_sem=r1.at[slot, i],
            device_id=peer(m),
            device_id_type=MESH,
        )

    def copy2(slot, i):
        b, m = plan.cross[i]
        mine = piece(2 ** min(b, k), 0)
        if b > k:
            target = recv2.at[slot, plan.slots2.index((b, m))]
        else:
            target = coef.at[slot, b, mine]
        return pltpu.make_async_remote_copy(
            src_ref=parts.at[slot, b, mine],
            dst_ref=target,
            send_sem=s2.at[slot, i],
            recv_sem=r2.at[slot, i],
            device_id=peer(plan.cross_mask(b, m)),
            device_id_type=MESH,
        )

    def copy3(slot, i):
        run, m = plan.first[i]
        b, count, group = plan.runs[run]
        mine = coef.at[slot, pl.ds(b, count), piece(group, 0)]
        return pltpu.make_async_remote_copy(
            src_ref=mine,
            dst_ref=mine,
            send_sem=s3.at[slot, i],
            recv_sem=r3.at[slot, i],
            device_id=peer(m),
            device_id_type=MESH,
        )

    def factor(node_rows):
        return 1.0 / math.sqrt(node_rows * level_count)

    def leaf_slice(g):
        return slice(g * leaf_rows, (g + 1) * leaf_rows)

    def project(slot, c):
        me_rows = slice(c * wide, (c + 1) * wide)
        top = levels
        while top > 0:
            low = max(top - 2, 0)
            group = list(range(low, top))
            total = None
            for g in range(leaf_count):
                cols = leaf_slice(g)
                weights = jnp.concatenate([v_up[b, cols, :] for b in group], axis=1)
                term = nn(o_ref[me_rows, cols], weights)
                total = term if total is None else total + term
            rank = total.shape[1] // len(group)
            for i, b in enumerate(group):
                parts[slot, b] = total[:, i * rank : (i + 1) * rank]
            for i, (run, m) in enumerate(plan.first):
                if low <= plan.runs[run][0] < top:
                    copy1(slot, i).start()
            top = low
        for i, (b, m) in enumerate(plan.cross):
            if b == 0:
                copy2(slot, i).start()

    def local_part(slot, c):
        me_rows = slice(c * wide, (c + 1) * wide)
        sums = []
        for g in range(leaf_count):
            cols = leaf_slice(g)
            weights = jnp.concatenate([v_loc[j, cols, :] for j in range(local_count)], axis=1)
            sums.append(nn(o_ref[me_rows, cols], weights))
        rank = sums[0].shape[1] // local_count
        for g in range(leaf_count):
            cols = leaf_slice(g)
            pieces = []
            for j in range(local_count):
                node = (g >> j) ^ 1
                total = None
                for h in range(node << j, (node + 1) << j):
                    term = sums[h][:, j * rank : (j + 1) * rank]
                    total = term if total is None else total + term
                pieces.append((total * factor(leaf_rows * 2**j)).astype(BF16))
            bases = jnp.concatenate([u_loc[j, cols, :] for j in range(local_count)], axis=1)
            acc[me_rows, cols] = nt(o_ref[me_rows, cols], leaves[cols, :]) + nt(
                jnp.concatenate(pieces, axis=1), bases
            )

    def reduce_send(slot):
        for run, (b, count, group) in enumerate(plan.runs):
            for i, (r, m) in enumerate(plan.first):
                if r == run:
                    copy1(slot, i).wait_recv()
            mine = piece(group, 0)
            total = parts[slot, pl.ds(b, count), mine, :]
            for m in range(1, group):
                total = total + recv1[run][slot, m - 1]
            parts[slot, pl.ds(b, count), mine, :] = total
            for i, (level, m) in enumerate(plan.cross):
                if b <= level < b + count:
                    copy2(slot, i).start()

    def cross_send(slot):
        for run, (b, count, group) in enumerate(plan.runs):
            for level in range(b, b + count):
                total = None
                for i, (other, m) in enumerate(plan.cross):
                    if other == level:
                        copy2(slot, i).wait_recv()
                        if level > k:
                            term = recv2[slot, plan.slots2.index((level, m))]
                            total = term if total is None else total + term
                if total is not None:
                    coef[slot, level, piece(group, 0), :] = total
            for i, (r, m) in enumerate(plan.first):
                if r == run:
                    copy3(slot, i).start()

    def finish(slot, c):
        me_rows = slice(c * wide, (c + 1) * wide)
        for i, (b, m) in enumerate(plan.cross):
            if b == 0:
                copy2(slot, i).wait_recv()
        for i in range(len(plan.first)):
            copy3(slot, i).wait_recv()
        scaled = jnp.concatenate(
            [(coef[slot, b] * factor(dev_rows * 2**b)).astype(BF16) for b in range(levels)],
            axis=1,
        )
        for g in range(leaf_count):
            cols = leaf_slice(g)
            bases = jnp.concatenate([u_up[b, cols, :] for b in range(levels)], axis=1)
            o_ref[me_rows, cols] = (acc[me_rows, cols] + nt(scaled, bases)).astype(BF16)
        for i in range(len(plan.first)):
            copy1(slot, i).wait_send()
            copy3(slot, i).wait_send()
        for i in range(len(plan.cross)):
            copy2(slot, i).wait_send()

    def body(it, carry):
        slots = [it * chunks + c for c in range(chunks)]
        for c in range(chunks):
            project(slots[c], c)

        @pl.when(it == 0)
        def _():
            for i in (1, 2, 3):
                loads[i].wait()

        for c in range(chunks):
            local_part(slots[c], c)
            reduce_send(slots[c])
        for c in range(chunks):
            cross_send(slots[c])

        @pl.when(it == 0)
        def _():
            loads[4].wait()

        for c in range(chunks):
            finish(slots[c], c)
        return carry

    lax.fori_loop(0, ITERS, body, 0)


def local(vectors, leaves, u_local, v_local, u_upper, v_upper):
    wide = vectors.shape[0]
    levels = u_upper.shape[0]
    rank = u_upper.shape[2]
    plan = Plan(levels, GROUP_BITS, wide // CHUNKS)
    slots = ITERS * CHUNKS
    n1, n2 = len(plan.first), len(plan.cross)
    big = plan.rows(2**plan.k)
    dma = pltpu.SemaphoreType.DMA
    scratch = [pltpu.VMEM(x.shape, x.dtype) for x in (leaves, u_local, v_local, u_upper, v_upper)]
    scratch += [
        pltpu.VMEM(vectors.shape, F32),
        pltpu.VMEM((slots, levels, plan.wide, rank), F32),
        pltpu.VMEM((slots, levels, plan.wide, rank), F32),
        pltpu.VMEM((slots, max(1, len(plan.slots2)), big, rank), F32),
    ]
    scratch += [
        pltpu.VMEM((slots, group - 1, count, plan.rows(group), rank), F32)
        for _, count, group in plan.runs
    ]
    scratch += [dma((6,)), dma((slots, n1)), dma((slots, n1)), dma((slots, n2)), dma((slots, n2))]
    scratch += [dma((slots, n1)), dma((slots, n1))]
    return pl.pallas_call(
        functools.partial(kernel, plan, lax.axis_size("lo"), CHUNKS, leaves.shape[1]),
        out_shape=jax.ShapeDtypeStruct(vectors.shape, vectors.dtype),
        in_specs=[pl.BlockSpec(memory_space=pl.ANY)] * 6,
        out_specs=pl.BlockSpec(memory_space=pltpu.VMEM),
        scratch_shapes=scratch,
        compiler_params=pltpu.CompilerParams(
            collective_id=0, has_side_effects=True, vmem_limit_bytes=56 * 2**20
        ),
    )(vectors, leaves, u_local, v_local, u_upper, v_upper)


def solution(mesh):
    return jax.shard_map(
        local,
        mesh=mesh,
        in_specs=(
            P(None, ("hi", "lo")),
            P(("hi", "lo"), None),
            P(None, ("hi", "lo"), None),
            P(None, ("hi", "lo"), None),
            P(None, ("hi", "lo"), None),
            P(None, ("hi", "lo"), None),
        ),
        out_specs=P(None, ("hi", "lo")),
        check_vma=False,
    )
```

time: 193 us -> 72.4 us (0.38)
  waiting for transfers between devices: 87.1 us -> 0 us
  Pallas kernels: 0 us -> 70.4 us
  local copies, waits for them, and re-layouts: 47 us -> 1.88 us
  matrix products: 31.7 us -> 0 us
  starting transfers between devices: 24.9 us -> 0 us
    ppermute x20 -> x0, waiting for transfers between devices: 87.1 us -> none  [from_partner(): return lax.ppermute(value, axis, pairs)]
    pallas_call x0 -> x1, Pallas kernels: none -> 70.4 us  [local(): pl.pallas_call(functools.partial(kernel, plan, lax.axis_size('lo'), CHUNK...]
    dot_general x28 -> x0, matrix products: 31.7 us -> none  [the longest x4 11.4 us: apply_operator(): jnp.einsum('bsr,bcr->cs', u_upper, coefs, preferred_element_type=jnp.floa...]
    ppermute x20 -> x0, starting transfers between devices: 24.9 us -> none  [from_partner(): return lax.ppermute(value, axis, pairs)]
    add x8 -> x0, local copies, waits for them, and re-layouts: 20.3 us -> none  [apply_operator(): result = result + added.reshape(wide, dev_rows)]
    reshape x4 -> x0, local copies, waits for them, and re-layouts: 10.2 us -> none  [apply_operator(): result = result + added.reshape(wide, dev_rows)]
    transpose x4 -> x0, local copies, waits for them, and re-layouts: 10.1 us -> none  [apply_operator(): jnp.einsum('gsr,gcr->cgs', u_local[level].reshape(groups, node_rows, rank...]
    another operation x4 -> x0, local copies, waits for them, and re-layouts: 3.38 us -> none  [apply_operator(): coefs = jnp.stack(lower_found + upper_found)]
  transfers between devices with their start and end apart: 20 -> 0, of which waited for: 16 -> 0; matrix products, arithmetic and copies ran while one was open for 28% -> 0% of each run, Pallas kernels for 0% -> 0%
where the time goes in v1:
time: 72.4 us; the launch traced here: 72.3 us
  Pallas kernels  70.4 us (97%)
  local copies, waits for them, and re-layouts  1.88 us (3%)
    pallas_call x1, Pallas kernels, local(): pl.pallas_call(functools.partial(kernel, plan, lax.axis_size('lo'), CHUNK...  70.4 us
    unnamed x1, local copies, waits for them, and re-layouts  1.88 us

profile of v1, /device:TPU:0, one launch (start us, length us, event | category | flops | bytes accessed | tf_op | source)
XLA Modules:
  0.0 72.3 jit_solution(3813471637575118603)
XLA Ops:
  0.0 70.4 %shard_map.64 = bf16[128,2048]{1,0:T(8,128)(2,1)} custom-call(bf16[128,2048]{1,0:T(8,128)(2,1)} %refs_0_.1, bf16[2048,512]{1,0:T(8,128)(2,1)} %refs_1_.1, bf16[2,2048,128]{2,1,0:T(8,128)(2,1)} %refs_2_.1, bf16[2,2048,128]{2,1,0:T(8,128)(2,1)} %refs_3_.1, bf16[5,2048,128]{2,1,0:T(8,128)(2,1)} %refs_4_.1, bf16[5,2048,128]{2,1,0:T(8,128)(2,1)} %refs_5_.1), custom_call_target="tpu_custom_call" | custom-call | tf_op jit(solution)/shard_map/pallas_call | solution.py:292
  70.4 1.9 %copy.8 = bf16[128,2048]{1,0:T(8,128)(2,1)} copy(bf16[128,2048]{1,0:T(8,128)(2,1)} %shard_map.64) | data formatting | bytes 1048576

commit v2 on v1

--- a/solution.py
+++ b/solution.py
@@ -9,8 +9,8 @@
 from jax.sharding import PartitionSpec as P
 
 ITERS = 4
-GROUP_BITS = 3
-CHUNKS = 1
+GROUP_BITS = 2
+CHUNKS = 2
 MESH = pl.DeviceIdType.MESH
 F32 = jnp.float32
 BF16 = jnp.bfloat16
@@ -162,9 +162,6 @@
                 if low <= plan.runs[run][0] < top:
                     copy1(slot, i).start()
             top = low
-        for i, (b, m) in enumerate(plan.cross):
-            if b == 0:
-                copy2(slot, i).start()
 
     def local_part(slot, c):
         me_rows = slice(c * wide, (c + 1) * wide)
@@ -202,6 +199,9 @@
             for i, (level, m) in enumerate(plan.cross):
                 if b <= level < b + count:
                     copy2(slot, i).start()
+        for i, (level, m) in enumerate(plan.cross):
+            if level == 0:
+                copy2(slot, i).start()
 
     def cross_send(slot):
         for run, (b, count, group) in enumerate(plan.runs):
@@ -234,16 +234,17 @@
             cols = leaf_slice(g)
             bases = jnp.concatenate([u_up[b, cols, :] for b in range(levels)], axis=1)
             o_ref[me_rows, cols] = (acc[me_rows, cols] + nt(scaled, bases)).astype(BF16)
+
+    def drain(slot, carry):
         for i in range(len(plan.first)):
             copy1(slot, i).wait_send()
             copy3(slot, i).wait_send()
         for i in range(len(plan.cross)):
             copy2(slot, i).wait_send()
+        return carry
 
     def body(it, carry):
         slots = [it * chunks + c for c in range(chunks)]
-        for c in range(chunks):
-            project(slots[c], c)
 
         @pl.when(it == 0)
         def _():
@@ -262,9 +263,17 @@
 
         for c in range(chunks):
             finish(slots[c], c)
+
+            @pl.when(it < ITERS - 1)
+            def _():
+                project(slots[c] + chunks, c)
+
         return carry
 
+    for c in range(chunks):
+        project(c, c)
     lax.fori_loop(0, ITERS, body, 0)
+    lax.fori_loop(0, ITERS * chunks, drain, 0)
 
 
 def local(vectors, leaves, u_local, v_local, u_upper, v_upper):

time: 72.4 us -> 65.6 us (0.906)
  Pallas kernels: 70.4 us -> 63.6 us
    pallas_call x1, Pallas kernels: 70.4 us -> 63.6 us  [local(): pl.pallas_call(functools.partial(kernel, plan, lax.axis_size('lo'), CHUNK...]
where the time goes in v2:
time: 65.6 us; the launch traced here: 65.5 us
  Pallas kernels  63.6 us (97%)
  local copies, waits for them, and re-layouts  1.88 us (3%)
    pallas_call x1, Pallas kernels, local(): pl.pallas_call(functools.partial(kernel, plan, lax.axis_size('lo'), CHUNK...  63.6 us
    unnamed x1, local copies, waits for them, and re-layouts  1.88 us

profile of v2, /device:TPU:0, one launch (start us, length us, event | category | flops | bytes accessed | tf_op | source)
XLA Modules:
  0.0 65.5 jit_solution(1706082395689575736)
XLA Ops:
  0.0 63.6 %shard_map.64 = bf16[128,2048]{1,0:T(8,128)(2,1)} custom-call(bf16[128,2048]{1,0:T(8,128)(2,1)} %refs_0_.1, bf16[2048,512]{1,0:T(8,128)(2,1)} %refs_1_.1, bf16[2,2048,128]{2,1,0:T(8,128)(2,1)} %refs_2_.1, bf16[2,2048,128]{2,1,0:T(8,128)(2,1)} %refs_3_.1, bf16[5,2048,128]{2,1,0:T(8,128)(2,1)} %refs_4_.1, bf16[5,2048,128]{2,1,0:T(8,128)(2,1)} %refs_5_.1), custom_call_target="tpu_custom_call" | custom-call | tf_op jit(solution)/shard_map/pallas_call | solution.py:301
  63.6 1.9 %copy.8 = bf16[128,2048]{1,0:T(8,128)(2,1)} copy(bf16[128,2048]{1,0:T(8,128)(2,1)} %shard_map.64) | data formatting | bytes 1048576

commit v3 on v2

--- a/solution.py
+++ b/solution.py
@@ -9,7 +9,6 @@
 from jax.sharding import PartitionSpec as P
 
 ITERS = 4
-GROUP_BITS = 2
 CHUNKS = 2
 MESH = pl.DeviceIdType.MESH
 F32 = jnp.float32
@@ -27,25 +26,48 @@
     return out
 
 
+def spread(index, bits):
+    return sum(1 << bit for i, bit in enumerate(bits) if (index >> i) & 1)
+
+
+def group_bits(level):
+    if level >= 4:
+        return (1, 2)
+    return tuple(range(min(level, 2)))
+
+
 class Plan:
-    def __init__(self, levels, group_bits, wide):
+    def __init__(self, levels, wide):
         self.levels = levels
-        self.k = min(group_bits, levels - 1)
         self.wide = wide
-        k = self.k
-        self.runs = [(b, 1, 2**b) for b in range(1, k)] + [(k, levels - k, 2**k)]
-        self.first = [(r, m) for r, run in enumerate(self.runs) for m in range(1, run[2])]
-        self.cross = [(b, m) for b in range(levels) for m in range(2 ** max(0, b - k))]
-        self.slots2 = [(b, m) for b, m in self.cross if b > k]
-
-    def rows(self, group):
-        return self.wide // group
+        self.runs = []
+        for b in range(1, levels):
+            if self.runs and self.runs[-1][2] == group_bits(b):
+                first, count, bits = self.runs[-1]
+                self.runs[-1] = (first, count + 1, bits)
+            else:
+                self.runs.append((b, 1, group_bits(b)))
+        self.first = [
+            (r, m) for r, run in enumerate(self.runs) for m in range(1, 2 ** len(run[2]))
+        ]
+        self.cross = [(b, m) for b in range(levels) for m in range(2 ** len(self.rest(b)))]
+        self.slots2 = [(b, m) for b, m in self.cross if self.rest(b)]
+
+    def rest(self, b):
+        return [bit for bit in range(b) if bit not in group_bits(b)]
+
+    def rows(self, bits):
+        return self.wide // 2 ** len(bits)
+
+    def first_mask(self, run, m):
+        return spread(m, self.runs[run][2])
 
     def cross_mask(self, b, m):
-        return (1 << b) ^ (m << self.k)
+        return (1 << b) ^ spread(m, self.rest(b))
 
     def partners(self):
-        masks = {m for _, m in self.first} | {self.cross_mask(b, m) for b, m in self.cross}
+        masks = {self.first_mask(r, m) for r, m in self.first}
+        masks |= {self.cross_mask(b, m) for b, m in self.cross}
         return sorted(masks)
 
 
@@ -63,7 +85,7 @@
     acc, parts, coef, recv2 = refs[12:16]
     recv1 = refs[16 : 16 + len(plan.runs)]
     load_sem, s1, r1, s2, r2, s3, r3 = refs[16 + len(plan.runs) :]
-    levels, k = plan.levels, plan.k
+    levels = plan.levels
     wide = plan.wide
     dev_rows = o_ref.shape[1]
     local_count = u_loc.shape[0]
@@ -91,27 +113,31 @@
     loads[5].wait()
     pl.semaphore_wait(barrier, len(masks))
 
-    def piece(group, mask):
-        rows = plan.rows(group)
-        index = flip(lax.rem(me, group), mask)
-        return pl.ds(pl.multiple_of(index * rows, 8), rows)
+    def piece(bits, mask):
+        rows = plan.rows(bits)
+        index = 0
+        for i, bit in enumerate(bits):
+            index = index + lax.rem(lax.div(me, 2**bit), 2) * 2**i
+        if not bits:
+            return pl.ds(0, rows)
+        return pl.ds(pl.multiple_of(flip(index, mask) * rows, 8), rows)
 
     def copy1(slot, i):
         run, m = plan.first[i]
-        b, count, group = plan.runs[run]
+        b, count, bits = plan.runs[run]
         return pltpu.make_async_remote_copy(
-            src_ref=parts.at[slot, pl.ds(b, count), piece(group, m)],
+            src_ref=parts.at[slot, pl.ds(b, count), piece(bits, m)],
             dst_ref=recv1[run].at[slot, m - 1],
             send_sem=s1.at[slot, i],
             recv_sem=r1.at[slot, i],
-            device_id=peer(m),
+            device_id=peer(plan.first_mask(run, m)),
             device_id_type=MESH,
         )
 
     def copy2(slot, i):
         b, m = plan.cross[i]
-        mine = piece(2 ** min(b, k), 0)
-        if b > k:
+        mine = piece(group_bits(b), 0)
+        if plan.rest(b):
             target = recv2.at[slot, plan.slots2.index((b, m))]
         else:
             target = coef.at[slot, b, mine]
@@ -126,14 +152,14 @@
 
     def copy3(slot, i):
         run, m = plan.first[i]
-        b, count, group = plan.runs[run]
-        mine = coef.at[slot, pl.ds(b, count), piece(group, 0)]
+        b, count, bits = plan.runs[run]
+        mine = coef.at[slot, pl.ds(b, count), piece(bits, 0)]
         return pltpu.make_async_remote_copy(
             src_ref=mine,
             dst_ref=mine,
             send_sem=s3.at[slot, i],
             recv_sem=r3.at[slot, i],
-            device_id=peer(m),
+            device_id=peer(plan.first_mask(run, m)),
             device_id_type=MESH,
         )
 
@@ -187,13 +213,13 @@
             )
 
     def reduce_send(slot):
-        for run, (b, count, group) in enumerate(plan.runs):
+        for run, (b, count, bits) in reversed(list(enumerate(plan.runs))):
             for i, (r, m) in enumerate(plan.first):
                 if r == run:
                     copy1(slot, i).wait_recv()
-            mine = piece(group, 0)
+            mine = piece(bits, 0)
             total = parts[slot, pl.ds(b, count), mine, :]
-            for m in range(1, group):
+            for m in range(1, 2 ** len(bits)):
                 total = total + recv1[run][slot, m - 1]
             parts[slot, pl.ds(b, count), mine, :] = total
             for i, (level, m) in enumerate(plan.cross):
@@ -204,17 +230,17 @@
                 copy2(slot, i).start()
 
     def cross_send(slot):
-        for run, (b, count, group) in enumerate(plan.runs):
+        for run, (b, count, bits) in enumerate(plan.runs):
             for level in range(b, b + count):
                 total = None
                 for i, (other, m) in enumerate(plan.cross):
                     if other == level:
                         copy2(slot, i).wait_recv()
-                        if level > k:
+                        if plan.rest(level):
                             term = recv2[slot, plan.slots2.index((level, m))]
                             total = term if total is None else total + term
                 if total is not None:
-                    coef[slot, level, piece(group, 0), :] = total
+                    coef[slot, level, piece(bits, 0), :] = total
             for i, (r, m) in enumerate(plan.first):
                 if r == run:
                     copy3(slot, i).start()
@@ -280,10 +306,10 @@
     wide = vectors.shape[0]
     levels = u_upper.shape[0]
     rank = u_upper.shape[2]
-    plan = Plan(levels, GROUP_BITS, wide // CHUNKS)
+    plan = Plan(levels, wide // CHUNKS)
     slots = ITERS * CHUNKS
     n1, n2 = len(plan.first), len(plan.cross)
-    big = plan.rows(2**plan.k)
+    big = plan.rows(group_bits(levels))
     dma = pltpu.SemaphoreType.DMA
     scratch = [pltpu.VMEM(x.shape, x.dtype) for x in (leaves, u_local, v_local, u_upper, v_upper)]
     scratch += [
@@ -293,8 +319,8 @@
         pltpu.VMEM((slots, max(1, len(plan.slots2)), big, rank), F32),
     ]
     scratch += [
-        pltpu.VMEM((slots, group - 1, count, plan.rows(group), rank), F32)
-        for _, count, group in plan.runs
+        pltpu.VMEM((slots, 2 ** len(bits) - 1, count, plan.rows(bits), rank), F32)
+        for _, count, bits in plan.runs
     ]
     scratch += [dma((6,)), dma((slots, n1)), dma((slots, n1)), dma((slots, n2)), dma((slots, n2))]
     scratch += [dma((slots, n1)), dma((slots, n1))]

time: 65.6 us -> 65 us (level)
  Pallas kernels: 63.6 us -> 62.9 us
where the time goes in v3:
time: 65 us; the launch traced here: 64.8 us
  Pallas kernels  62.9 us (97%)
  local copies, waits for them, and re-layouts  1.88 us (3%)
    pallas_call x1, Pallas kernels, local(): pl.pallas_call(functools.partial(kernel, plan, lax.axis_size('lo'), CHUNK...  62.9 us
    unnamed x1, local copies, waits for them, and re-layouts  1.88 us

profile of v3, /device:TPU:0, one launch (start us, length us, event | category | flops | bytes accessed | tf_op | source)
XLA Modules:
  0.0 64.8 jit_solution(1294955223149697142)
XLA Ops:
  0.0 62.9 %shard_map.64 = bf16[128,2048]{1,0:T(8,128)(2,1)} custom-call(bf16[128,2048]{1,0:T(8,128)(2,1)} %refs_0_.1, bf16[2048,512]{1,0:T(8,128)(2,1)} %refs_1_.1, bf16[2,2048,128]{2,1,0:T(8,128)(2,1)} %refs_2_.1, bf16[2,2048,128]{2,1,0:T(8,128)(2,1)} %refs_3_.1, bf16[5,2048,128]{2,1,0:T(8,128)(2,1)} %refs_4_.1, bf16[5,2048,128]{2,1,0:T(8,128)(2,1)} %refs_5_.1), custom_call_target="tpu_custom_call" | custom-call | tf_op jit(solution)/shard_map/pallas_call | solution.py:327
  62.9 1.9 %copy.8 = bf16[128,2048]{1,0:T(8,128)(2,1)} copy(bf16[128,2048]{1,0:T(8,128)(2,1)} %shard_map.64) | data formatting | bytes 1048576

commit v4 on v3

--- a/solution.py
+++ b/solution.py
@@ -71,10 +71,6 @@
         return sorted(masks)
 
 
-def nt(a, b):
-    return lax.dot_general(a, b, (((1,), (1,)), ((), ())), preferred_element_type=F32)
-
-
 def nn(a, b):
     return jnp.dot(a, b, preferred_element_type=F32)
 
@@ -83,8 +79,9 @@
     hbm, o_ref = refs[:6], refs[6]
     leaves, u_loc, v_loc, u_up, v_up = refs[7:12]
     acc, parts, coef, recv2 = refs[12:16]
-    recv1 = refs[16 : 16 + len(plan.runs)]
-    load_sem, s1, r1, s2, r2, s3, r3 = refs[16 + len(plan.runs) :]
+    leaves_t, u_loc_t, u_up_t = refs[16:19]
+    recv1 = refs[19 : 19 + len(plan.runs)]
+    load_sem, s1, r1, s2, r2, s3, r3 = refs[19 + len(plan.runs) :]
     levels = plan.levels
     wide = plan.wide
     dev_rows = o_ref.shape[1]
@@ -168,6 +165,13 @@
 
     def leaf_slice(g):
         return slice(g * leaf_rows, (g + 1) * leaf_rows)
+
+    def turn(source, target):
+        rank = source.shape[2]
+        for b in range(source.shape[0]):
+            for g in range(leaf_count):
+                cols = leaf_slice(g)
+                target[b * rank : (b + 1) * rank, cols] = source[b, cols, :].T
 
     def project(slot, c):
         me_rows = slice(c * wide, (c + 1) * wide)
@@ -207,9 +211,8 @@
                     term = sums[h][:, j * rank : (j + 1) * rank]
                     total = term if total is None else total + term
                 pieces.append((total * factor(leaf_rows * 2**j)).astype(BF16))
-            bases = jnp.concatenate([u_loc[j, cols, :] for j in range(local_count)], axis=1)
-            acc[me_rows, cols] = nt(o_ref[me_rows, cols], leaves[cols, :]) + nt(
-                jnp.concatenate(pieces, axis=1), bases
+            acc[me_rows, cols] = nn(o_ref[me_rows, cols], leaves_t[:, cols]) + nn(
+                jnp.concatenate(pieces, axis=1), u_loc_t[:, cols]
             )
 
     def reduce_send(slot):
@@ -258,8 +261,7 @@
         )
         for g in range(leaf_count):
             cols = leaf_slice(g)
-            bases = jnp.concatenate([u_up[b, cols, :] for b in range(levels)], axis=1)
-            o_ref[me_rows, cols] = (acc[me_rows, cols] + nt(scaled, bases)).astype(BF16)
+            o_ref[me_rows, cols] = (acc[me_rows, cols] + nn(scaled, u_up_t[:, cols])).astype(BF16)
 
     def drain(slot, carry):
         for i in range(len(plan.first)):
@@ -276,6 +278,10 @@
         def _():
             for i in (1, 2, 3):
                 loads[i].wait()
+            for g in range(leaf_count):
+                cols = leaf_slice(g)
+                leaves_t[:, cols] = leaves[cols, :].T
+            turn(u_loc, u_loc_t)
 
         for c in range(chunks):
             local_part(slots[c], c)
@@ -286,6 +292,7 @@
         @pl.when(it == 0)
         def _():
             loads[4].wait()
+            turn(u_up, u_up_t)
 
         for c in range(chunks):
             finish(slots[c], c)
@@ -317,6 +324,12 @@
         pltpu.VMEM((slots, levels, plan.wide, rank), F32),
         pltpu.VMEM((slots, levels, plan.wide, rank), F32),
         pltpu.VMEM((slots, max(1, len(plan.slots2)), big, rank), F32),
+    ]
+    dev_rows = vectors.shape[1]
+    scratch += [
+        pltpu.VMEM((leaves.shape[1], dev_rows), BF16),
+        pltpu.VMEM((u_local.shape[0] * rank, dev_rows), BF16),
+        pltpu.VMEM((levels * rank, dev_rows), BF16),
     ]
     scratch += [
         pltpu.VMEM((slots, 2 ** len(bits) - 1, count, plan.rows(bits), rank), F32)

time: 65 us -> 63.6 us (0.978)
  Pallas kernels: 62.9 us -> 61.6 us
    pallas_call x1, Pallas kernels: 62.9 us -> 61.6 us  [local(): pl.pallas_call(functools.partial(kernel, plan, lax.axis_size('lo'), CHUNK...]
where the time goes in v4:
time: 63.6 us; the launch traced here: 63.5 us
  Pallas kernels  61.6 us (97%)
  local copies, waits for them, and re-layouts  1.88 us (3%)
    pallas_call x1, Pallas kernels, local(): pl.pallas_call(functools.partial(kernel, plan, lax.axis_size('lo'), CHUNK...  61.6 us
    unnamed x1, local copies, waits for them, and re-layouts  1.88 us

profile of v4, /device:TPU:0, one launch (start us, length us, event | category | flops | bytes accessed | tf_op | source)
XLA Modules:
  0.0 63.5 jit_solution(8751606234899593585)
XLA Ops:
  0.0 61.6 %shard_map.64 = bf16[128,2048]{1,0:T(8,128)(2,1)} custom-call(bf16[128,2048]{1,0:T(8,128)(2,1)} %refs_0_.1, bf16[2048,512]{1,0:T(8,128)(2,1)} %refs_1_.1, bf16[2,2048,128]{2,1,0:T(8,128)(2,1)} %refs_2_.1, bf16[2,2048,128]{2,1,0:T(8,128)(2,1)} %refs_3_.1, bf16[5,2048,128]{2,1,0:T(8,128)(2,1)} %refs_4_.1, bf16[5,2048,128]{2,1,0:T(8,128)(2,1)} %refs_5_.1), custom_call_target="tpu_custom_call" | custom-call | tf_op jit(solution)/shard_map/pallas_call | solution.py:340
  61.6 1.9 %copy.8 = bf16[128,2048]{1,0:T(8,128)(2,1)} copy(bf16[128,2048]{1,0:T(8,128)(2,1)} %shard_map.64) | data formatting | bytes 1048576

commit v5 on v4

--- a/solution.py
+++ b/solution.py
@@ -9,7 +9,7 @@
 from jax.sharding import PartitionSpec as P
 
 ITERS = 4
-CHUNKS = 2
+CHUNKS = 1
 MESH = pl.DeviceIdType.MESH
 F32 = jnp.float32
 BF16 = jnp.bfloat16

time: 63.6 us -> 65.7 us (1.033)
  Pallas kernels: 61.6 us -> 63.6 us
    pallas_call x1, Pallas kernels: 61.6 us -> 63.6 us  [local(): pl.pallas_call(functools.partial(kernel, plan, lax.axis_size('lo'), CHUNK...]
where the time goes in v5:
time: 65.7 us; the launch traced here: 65.5 us
  Pallas kernels  63.6 us (97%)
  local copies, waits for them, and re-layouts  1.88 us (3%)
    pallas_call x1, Pallas kernels, local(): pl.pallas_call(functools.partial(kernel, plan, lax.axis_size('lo'), CHUNK...  63.6 us
    unnamed x1, local copies, waits for them, and re-layouts  1.88 us

profile of v5, /device:TPU:0, one launch (start us, length us, event | category | flops | bytes accessed | tf_op | source)
XLA Modules:
  0.0 65.5 jit_solution(6787980492816289175)
XLA Ops:
  0.0 63.6 %shard_map.64 = bf16[128,2048]{1,0:T(8,128)(2,1)} custom-call(bf16[128,2048]{1,0:T(8,128)(2,1)} %refs_0_.1, bf16[2048,512]{1,0:T(8,128)(2,1)} %refs_1_.1, bf16[2,2048,128]{2,1,0:T(8,128)(2,1)} %refs_2_.1, bf16[2,2048,128]{2,1,0:T(8,128)(2,1)} %refs_3_.1, bf16[5,2048,128]{2,1,0:T(8,128)(2,1)} %refs_4_.1, bf16[5,2048,128]{2,1,0:T(8,128)(2,1)} %refs_5_.1), custom_call_target="tpu_custom_call" | custom-call | tf_op jit(solution)/shard_map/pallas_call | solution.py:340
  63.6 1.9 %copy.8 = bf16[128,2048]{1,0:T(8,128)(2,1)} copy(bf16[128,2048]{1,0:T(8,128)(2,1)} %shard_map.64) | data formatting | bytes 1048576
